TPU v7x, 32 devices: a whole 2x2x4 slice. The times are simulated.
32 devices in a mesh: batch: 8 (over y, x, core), lib: 4 (over z).
Axes of the slice: x: 2, y: 2, z: 4, core: 2. Of those that a mesh axis runs over, the one named last changes fastest.
Arguments:
- skip_features: bfloat16 [64, 1024, 320], P(('batch', 'lib')), may hold values from -6 to 6
- cached_deep_features: bfloat16 [64, 1024, 640], P('lib', 'batch'), may hold values from -6 to 6
- target_position: int32 [4, 16], P('lib'), may hold values from 0 to 15, each once within a row
- request_adapter: int32 [64], P(('batch', 'lib')), may hold values from 0 to 15
- library_adapter: int32 [16], P('lib'), may hold values from 0 to 15, each once
- adapter_down_weight: bfloat16 [16, 64, 960], P('lib'), may hold values from -0.1875 to 0.1875
- adapter_up_weight: bfloat16 [16, 64, 320], P('lib'), may hold values from -0.75 to 0.75
- kernel_weight: bfloat16 [3, 3, 960, 320], replicated, may hold values from -0.0625 to 0.0625
- shortcut_matrix: bfloat16 [960, 320], replicated, may hold values from -0.1875 to 0.1875
- group_norm_gain: float32 [960], replicated, may hold values from 0.5 to 1.5
- group_norm_offset: float32 [960], replicated, may hold values from -1.8 to 1.8
- output_bias: float32 [320], replicated, may hold values from -1.8 to 1.8
Outputs:
- block_out: bfloat16 [64, 1024, 320], P(('batch', 'lib'))
Inputs may be any that keep to these rules, and one draw needn't show every extreme that they name: Each row of target_position names every one of its 16 slots once. `request_adapter`: ids of adapters in the library. `library_adapter`: every adapter id is held in exactly one library slot.
All inputs are finite; a program needn't handle non-finite values.
Results may differ from a plain program's by a relative error of at most 0.0045.
Values may be sent and summed in bfloat16 or wider, within the bound.
A program may use at most 128 MiB of HBM per device.

v0:
```python
import jax
import jax.numpy as jnp
from jax import lax
from jax.sharding import PartitionSpec as P

DEEP = 640
GROUPS = 32
ROWS = 32
LAT_W = 32


def norm_silu(joined, group_norm_gain, group_norm_offset):
    count = joined.shape[0]
    places = joined.shape[1]
    width = joined.shape[2]
    values = joined.astype(jnp.float32).reshape(count, places, GROUPS, width // GROUPS)
    center = jnp.mean(values, axis=(1, 3), keepdims=True)
    spread = jnp.mean((values - center) ** 2, axis=(1, 3), keepdims=True)
    scaled = ((values - center) / jnp.sqrt(spread + 1e-05)).reshape(
        count, places, width
    ) * group_norm_gain + group_norm_offset
    return jax.nn.silu(scaled).astype(jnp.bfloat16)


def local(
    skip_features,
    cached_deep_features,
    target_position,
    request_adapter,
    library_adapter,
    adapter_down_weight,
    adapter_up_weight,
    kernel_weight,
    shortcut_matrix,
    group_norm_gain,
    group_norm_offset,
    output_bias,
):
    batch_count = lax.axis_size("batch")
    per_device = skip_features.shape[0]
    places = skip_features.shape[1]
    column = target_position.shape[1]
    width = kernel_weight.shape[2]
    outputs = kernel_weight.shape[3]
    placing = target_position[0]
    inverse = jnp.zeros((column,), jnp.int32).at[placing].set(jnp.arange(column, dtype=jnp.int32))
    order = inverse.reshape(batch_count, per_device).T
    outgoing = cached_deep_features[order]
    arrived = lax.all_to_all(outgoing, "batch", split_axis=1, concat_axis=1, tiled=True)
    deep = arrived.reshape(per_device, places, DEEP)
    down_portion = lax.all_gather(adapter_down_weight, "lib", axis=0, tiled=True)
    up_portion = lax.all_gather(adapter_up_weight, "lib", axis=0, tiled=True)
    id_piece = lax.all_gather(library_adapter, "lib", axis=0, tiled=True)
    picker = (request_adapter[:, None] == id_piece[None, :]).astype(jnp.bfloat16)
    down_sum = jnp.einsum("rk,kij->rij", picker, down_portion, preferred_element_type=jnp.float32)
    up_sum = jnp.einsum("rk,kij->rij", picker, up_portion, preferred_element_type=jnp.float32)
    down_sum, up_sum = (down_sum, up_sum)
    down_blocks = down_sum.astype(jnp.bfloat16)
    up_blocks = up_sum.astype(jnp.bfloat16)
    joined = jnp.concatenate([skip_features, deep], axis=2)
    normed = norm_silu(joined, group_norm_gain, group_norm_offset)
    padded = jnp.pad(
        normed.reshape(per_device, ROWS, LAT_W, width), ((0, 0), (1, 1), (1, 1), (0, 0))
    )
    conv = jnp.zeros((per_device * places, outputs), jnp.float32)
    for row_off in range(3):
        for col_off in range(3):
            window = padded[:, row_off : row_off + ROWS, col_off : col_off + LAT_W].reshape(
                per_device * places, width
            )
            conv = conv + jnp.dot(
                window, kernel_weight[row_off, col_off], preferred_element_type=jnp.float32
            )
    shortcut = jnp.dot(
        joined.reshape(per_device * places, width),
        shortcut_matrix,
        preferred_element_type=jnp.float32,
    )
    low = jnp.einsum(
        "rpc,rkc->rpk", normed, down_blocks, preferred_element_type=jnp.float32
    ).astype(jnp.bfloat16)
    delta = jnp.einsum("rpk,rko->rpo", low, up_blocks, preferred_element_type=jnp.float32)
    total = (shortcut + conv).reshape(per_device, places, outputs) + output_bias + delta
    return total.astype(jnp.bfloat16)


def solution(mesh):
    in_specs = (
        P(("batch", "lib"), None, None),
        P("lib", "batch", None),
        P("lib", None),
        P(("batch", "lib")),
        P("lib"),
        P("lib", None, None),
        P("lib", None, None),
        P(),
        P(),
        P(),
        P(),
        P(),
    )
    out_specs = P(("batch", "lib"), None, None)
    return jax.shard_map(local, mesh=mesh, in_specs=in_specs, out_specs=out_specs, check_vma=False)
```

profile of v0, /device:TPU:0, one launch (start us, length us, event | category | flops | bytes accessed | tf_op | source)
XLA Modules:
  0.0 148.1 jit_solution(5434966734072437644)
XLA Ops:
  6.5 0.0 copy-start
  6.5 0.8 fusion.48
  7.3 0.6 scatter_custom_fusion
  8.0 0.1 reshape.168
  8.1 0.1 copy.33
  8.1 0.1 reshape.181
  8.2 0.1 copy-done
  8.3 2.4 %gather_fusion = bf16[16,128,640]{2,1,0:T(8,128)(2,1)} fusion(bf16[16,128,640]{2,1,0:T(8,128)(2,1)S(1)} %copy-done, s32[1024]{0:T(1024)S(1)} %pad_clamp_fusion), kind=kCustom, calls=%fused_computation | custom fusion | bytes 5242944 | tf_op jit(solution)/shard_map/gather | solution.py:48
  10.7 3.6 %copy.34 = bf16[2,8,128,640]{3,2,0,1:T(8,128)(2,1)} copy(bf16[2,8,128,640]{3,2,1,0:T(8,128)(2,1)} %bitcast.86) | data formatting | bytes 5242880 | tf_op jit(solution)/shard_map/gather | solution.py:48
  14.3 0.0 copy-start.14
  14.3 5.3 %all-to-all-start = ((bf16[2,8,128,640]{3,2,0,1:T(8,128)(2,1)}), bf16[2,8,128,640]{3,2,0,1:T(8,128)(2,1)}, u32[]{:S(2)}, u32[]{:S(2)}) async-start(bf16[2,8,128,640]{3,2,0,1:T(8,128)(2,1)} %copy.34), calls=%async_computation | async-start | bytes 5242880 | tf_op jit(solution)/shard_map/all_to_all | solution.py:49
  19.6 0.0 all-gather.2.cloned.1.call-start
  19.6 0.7 all-gather.2.cloned.1.call-update
  20.3 0.0 copy-done.9
  20.3 1.6 %copy.49 = bf16[2,1024,320]{2,1,0:T(8,128)(2,1)} copy(bf16[2,1024,320]{1,2,0:T(8,128)(2,1)S(1)} %copy-done.9) | data formatting | bytes 2621440 | tf_op jit(solution)/shard_map/concatenate | solution.py:60
  21.9 0.0 copy-done.17
  21.9 0.6 dynamic-slice
  23.2 0.2 dynamic-update-slice
  23.4 9.2 %all-reduce.1 = s32[16]{0:T(128)S(1)} all-reduce(s32[16]{0:T(128)S(1)} %dynamic-update-slice), channel_id=1, replica_groups=mesh['batch'=8,'lib'=4] {'lib'}, use_global_device_ids=true, to_apply=%add.1 | all-reduce | flops 16 | bytes 128
  32.6 0.0 copy-done.10
  32.6 29.5 %all_gather.11 = bf16[16,64,320]{2,1,0:T(8,128)(2,1)S(1)} all-gather(bf16[4,64,320]{2,1,0:T(8,128)(2,1)S(1)} %copy-done.10), channel_id=1, replica_groups=mesh['batch'=8,'lib'=4] {'lib'}, dimensions={0}, use_global_device_ids=true | all-gather | bytes 819200 | tf_op jit(solution)/shard_map/all_gather | solution.py:52
  62.1 0.0 copy-done.14
  62.1 0.5 convolution_convert_fusion.1
  62.7 0.0 all-to-all-done
  62.7 0.0 copy-start.2
  62.7 2.2 %copy.35 = bf16[2,8,128,640]{3,2,1,0:T(8,128)(2,1)S(1)} copy(bf16[2,8,128,640]{3,2,0,1:T(8,128)(2,1)} %all-to-all-done) | data formatting | bytes 5242880 | tf_op jit(solution)/shard_map/all_to_all | solution.py:49
  64.9 0.0 copy-start.11
  64.9 0.0 copy-start.12
  64.9 1.7 %convert_reduce_fusion = f32[2,960]{1,0:T(2,128)S(1)} fusion(bf16[2,1024,640]{2,1,0:T(8,128)(2,1)S(1)} %bitcast.72, bf16[2,1024,320]{2,1,0:T(8,128)(2,1)S(1)} %copy-done.2), kind=kLoop, calls=%fused_computation.3 | loop fusion | flops 9828480 | bytes 3939840 | tf_op jit(solution)/shard_map/reduce_sum | solution.py:17
  66.7 0.1 reduce_sum.24
  66.8 0.1 reduce_sum.25
  66.9 0.1 sub.31
  66.9 0.1 sub.32
  67.1 3.6 %fusion.2 = f32[2,960]{1,0:T(2,128)S(1)} fusion(f32[2,960]{1,0:T(2,128)S(1)} %sub.32, bf16[2,1024,640]{2,1,0:T(8,128)(2,1)S(1)} %bitcast.73, bf16[2,1024,320]{2,1,0:T(8,128)(2,1)} %copy.49), kind=kLoop, calls=%fused_computation.6 | loop fusion | flops 13760640 | bytes 3947520 | tf_op jit(solution)/shard_map/reduce_sum | solution.py:18
  70.7 0.1 reduce_sum.36
  70.8 0.1 reduce_sum.37
  70.9 0.1 div.49
  70.9 0.1 div.50
  71.1 0.0 copy-done.11
  71.1 6.8 %multiply_convert_fusion = bf16[2,1024,960]{2,1,0:T(8,128)(2,1)} fusion(f32[960]{0:T(1024)S(1)} %copy-done.11, f32[960]{0:T(1024)S(1)} %copy-done.12, f32[2,960]{1,0:T(2,128)S(1)} %div.50, f32[2,960]{1,0:T(2,128)S(1)} %sub.32, bf16[2,1024,640]{2,1,0:T(8,128)(2,1)S(1)} %bitcast.74, bf16[2,1024,320]{2,1,0:T(8,128)(2,1)} %copy.49), kind=kLoop, calls=%fused_computation.9 | loop fusion | flops 25559040 | bytes 7887360 | tf_op jit(solution)/shard_map/convert_element_type | solution.py:22
  77.9 5.6 %multiply_convert_fusion.1 = bf16[2,32,32,960]{3,2,1,0:T(8,128)(2,1)} fusion(bf16[2,32,32,640]{3,2,1,0:T(8,128)(2,1)S(1)} %bitcast.75, bf16[2,32,32,320]{3,2,1,0:T(8,128)(2,1)S(1)} %bitcast.77, f32[960]{0:T(1024)S(1)} %copy-done.11, f32[960]{0:T(1024)S(1)} %copy-done.12, f32[2,960]{1,0:T(2,128)S(1)} %div.50, f32[2,960]{1,0:T(2,128)S(1)} %sub.32), kind=kLoop, calls=%fused_computation.10 | loop fusion | flops 25559040 | bytes 7887360 | tf_op jit(solution)/shard_map/convert_element_type | solution.py:22
  83.5 22.2 %pad_slice_fusion = (bf16[2,32,32,960]{3,2,1,0:T(8,128)(2,1)S(1)}, bf16[2,32,32,960]{3,2,1,0:T(8,128)(2,1)}, bf16[2,32,32,960]{3,2,1,0:T(8,128)(2,1)}, bf16[2,32...) fusion(bf16[2,32,32,960]{3,2,1,0:T(8,128)(2,1)} %multiply_conve, ...), kind=kLoop, calls=%fused_computation.11 | loop fusion | bytes 35389440 | tf_op jit(solution)/shard_map/slice | solution.py:68
  105.8 0.0 slice-start
  105.8 4.1 %fusion.30 = f32[2048,320]{0,1:T(8,128)S(1)} fusion(bf16[2048,960]{1,0:T(8,128)(2,1)} %bitcast.88, bf16[3,3,960,320]{2,3,1,0:T(8,128)(2,1)} %param.19), kind=kOutput, calls=%fused_computation.51 | convolution fusion | flops 1258291200 | bytes 7471104 | tf_op jit(solution)/shard_map/dot_general | solution.py:71
  109.9 0.0 slice-start.1
  109.9 2.8 %convolution_add_fusion.6 = f32[2048,320]{0,1:T(8,128)S(1)} fusion(f32[2048,320]{0,1:T(8,128)S(1)} %fusion.30, bf16[2048,960]{1,0:T(8,128)(2,1)S(1)} %bitcast.84, bf16[3,3,960,320]{2,3,1,0:T(8,128)(2,1)} %param.19), kind=kOutput, calls=%fused_computation.32 | convolution fusion | flops 1258946560 | bytes 9830400 | tf_op jit(solution)/shard_map/dot_general | solution.py:71
  112.7 0.0 slice-done
  112.7 0.0 copy-done.5
  112.7 0.2 slice-done.1
  112.9 1.6 %convolution_add_fusion.5 = f32[2048,320]{0,1:T(8,128)S(1)} fusion(f32[2048,320]{0,1:T(8,128)S(1)} %convolution_add_fusion.6, bf16[2048,960]{1,0:T(8,128)(2,1)S(1)} %bitcast.83, bf16[3,3,960,320]{2,3,1,0:T(8,128)(2,1)S(1)} %bitcast.90), kind=kOutput, calls=%fused_computation.31 | convolution fusion | flops 1258946560 | bytes 10092544 | tf_op jit(solution)/shard_map/dot_general | solution.py:71
  114.5 0.6 copy-done.4
  115.1 1.6 %convolution_add_fusion.4 = f32[2048,320]{0,1:T(8,128)S(1)} fusion(f32[2048,320]{0,1:T(8,128)S(1)} %convolution_add_fusion.5, bf16[2048,960]{1,0:T(8,128)(2,1)S(1)} %bitcast.82, bf16[3,3,960,320]{2,3,1,0:T(8,128)(2,1)S(1)} %bitcast.90), kind=kOutput, calls=%fused_computation.30 | convolution fusion | flops 1258946560 | bytes 10092544 | tf_op jit(solution)/shard_map/dot_general | solution.py:71
  116.7 0.6 copy-done.8
  117.3 3.1 %fusion.24 = f32[2048,320]{0,1:T(8,128)} fusion(bf16[2048,960]{1,0:T(8,128)(2,1)S(1)} %bitcast.87, bf16[3,3,960,320]{2,3,1,0:T(8,128)(2,1)S(1)} %bitcast.90), kind=kOutput, calls=%fused_computation.45 | convolution fusion | flops 1258291200 | bytes 7471104 | tf_op jit(solution)/shard_map/dot_general | solution.py:71
  120.4 3.5 %fusion.12 = f32[2048,320]{0,1:T(8,128)S(1)} fusion(f32[2048,320]{0,1:T(8,128)} %fusion.24, f32[2048,320]{0,1:T(8,128)S(1)} %convolution_add_fusion.4, bf16[2048,960]{1,0:T(8,128)(2,1)S(1)} %bitcast.85, bf16[3,3,960,320]{2,3,1,0:T(8,128)(2,1)S(1)} %bitcast.90), kind=kOutput, calls=%fused_computation.26 | convolution fusion | flops 1259601920 | bytes 12713984 | tf_op jit(solution)/shard_map/dot_general | solution.py:71
  123.9 1.6 %convolution_add_fusion.3 = f32[2048,320]{0,1:T(8,128)S(1)} fusion(f32[2048,320]{0,1:T(8,128)S(1)} %fusion.12, bf16[2048,960]{1,0:T(8,128)(2,1)S(1)} %bitcast.81, bf16[3,3,960,320]{2,3,1,0:T(8,128)(2,1)S(1)} %bitcast.90), kind=kOutput, calls=%fused_computation.29 | convolution fusion | flops 1258946560 | bytes 10092544 | tf_op jit(solution)/shard_map/dot_general | solution.py:71
  125.5 1.6 %convolution_add_fusion.2 = f32[2048,320]{0,1:T(8,128)S(1)} fusion(f32[2048,320]{0,1:T(8,128)S(1)} %convolution_add_fusion.3, bf16[2048,960]{1,0:T(8,128)(2,1)S(1)} %bitcast.80, bf16[3,3,960,320]{2,3,1,0:T(8,128)(2,1)S(1)} %bitcast.90), kind=kOutput, calls=%fused_computation.28 | convolution fusion | flops 1258946560 | bytes 10092544 | tf_op jit(solution)/shard_map/dot_general | solution.py:71
  127.2 0.0 copy-start.15
  127.2 1.9 %convolution_add_fusion.1 = f32[2048,320]{0,1:T(8,128)S(1)} fusion(f32[2048,320]{0,1:T(8,128)S(1)} %convolution_add_fusion.2, bf16[2048,960]{1,0:T(8,128)(2,1)S(1)} %bitcast.79, bf16[3,3,960,320]{2,3,1,0:T(8,128)(2,1)S(1)} %bitcast.90), kind=kOutput, calls=%fused_computation.27 | convolution fusion | flops 1258946560 | bytes 10092544 | tf_op jit(solution)/shard_map/dot_general | solution.py:71
  129.1 0.0 copy-start.13
  129.1 3.3 %fusion.9 = f32[2048,320]{0,1:T(8,128)} fusion(f32[2048,320]{0,1:T(8,128)S(1)} %convolution_add_fusion.1, bf16[960,320]{0,1:T(8,128)(2,1)S(1)} %copy-done.15, bf16[2048,640]{1,0:T(8,128)(2,1)S(1)} %bitcast.76, bf16[2048,320]{1,0:T(8,128)(2,1)S(1)} %bitcast.78), kind=kOutput, calls=%fused_computation.24 | convolution fusion | flops 1266810880 | bytes 9789440 | tf_op jit(solution)/shard_map/dot_general | solution.py:74
  132.4 2.9 %fusion.17 = bf16[2,64,960]{2,0,1:T(2,128)(2,1)S(1)} fusion(bf16[16,64,960]{2,1,0:T(8,128)(2,1)} %all-gather.2.cloned.1.call-done, s32[16]{0:T(128)S(1)} %all-reduce.1, s32[2]{0:T(128)S(1)} %copy-done.14), kind=kOutput, calls=%fused_computation.39 | convolution fusion | flops 4055072 | bytes 2211912 | tf_op jit(solution)/shard_map/rk,kij->rij/dot_general | solution.py:55
  135.3 0.0 copy-start.1
  135.3 6.0 %fusion.14 = bf16[2,1024,320]{1,2,0:T(8,128)(2,1)} fusion(f32[40,2,8,1024]{3,2,1,0:T(8,128)} %bitcast.91, f32[320]{0:T(512)S(1)} %copy-done.13, bf16[2,1024,960]{2,1,0:T(8,128)(2,1)} %multiply_convert_fusion, bf16[2,64,960]{2,0,1:T(2,128)(2,1)S(1)} %fusion.17, bf16[2,64,320]{2,0,1:T(2,128)(2,1)S(1)} %convolution_convert_fusion.1), kind=kOutput, calls=%fused_computation.35 | convolution fusion | flops 337641472 | bytes 8193280 | tf_op jit(solution)/shard_map/rpk,rko->rpo/dot_general | solution.py:82
  (27 shorter events, 0.1 us)
Async XLA Ops:
  6.5 1.8 %copy-start = (bf16[16,128,640]{2,1,0:T(8,128)(2,1)S(1)}, bf16[16,128,640]{2,1,0:T(8,128)(2,1)}, u32[]{:S(2)}) copy-start(bf16[16,128,640]{2,1,0:T(8,128)(2,1)} %param.13) | copy-start | bytes 7864324
  14.3 6.1 %copy-start.9 = (bf16[2,1024,320]{1,2,0:T(8,128)(2,1)S(1)}, bf16[2,1024,320]{1,2,0:T(8,128)(2,1)}, u32[]{:S(2)}) copy-start(bf16[2,1024,320]{1,2,0:T(8,128)(2,1)} %param.12) | copy-start | bytes 3932164
  14.3 7.7 %copy-start.17 = (u32[32]{0:T(128)S(1)}, u32[32]{0:T(128)}, u32[]{:S(2)}) copy-start(u32[32]{0:T(128)} %constant.27) | copy-start | bytes 388
  14.3 8.9 %copy-start.16 = (s32[4]{0:T(128)S(1)}, s32[4]{0:T(128)}, u32[]{:S(2)}) copy-start(s32[4]{0:T(128)} %param.16) | copy-start | bytes 52
  14.3 18.3 %copy-start.10 = (bf16[4,64,320]{2,1,0:T(8,128)(2,1)S(1)}, bf16[4,64,320]{2,1,0:T(8,128)(2,1)}, u32[]{:S(2)}) copy-start(bf16[4,64,320]{2,1,0:T(8,128)(2,1)} %param.18) | copy-start | bytes 491524
  14.3 47.8 %copy-start.14 = (s32[2]{0:T(128)S(1)}, s32[2]{0:T(128)}, u32[]{:S(2)}) copy-start(s32[2]{0:T(128)} %param.15) | copy-start | bytes 28
  14.3 48.4 %all-to-all-start = ((bf16[2,8,128,640]{3,2,0,1:T(8,128)(2,1)}), bf16[2,8,128,640]{3,2,0,1:T(8,128)(2,1)}, u32[]{:S(2)}, u32[]{:S(2)}) async-start(bf16[2,8,128,640]{3,2,0,1:T(8,128)(2,1)} %copy.34), calls=%async_computation | async-start | bytes 5242880 | tf_op jit(solution)/shard_map/all_to_all | solution.py:49
  19.6 112.8 %all-gather.2.cloned.1.call-start = ((), (), s32[]{:S(2)}) async-start(), calls=%async_computation.1 | async-start | bytes 2621440 | tf_op jit(solution)/shard_map/all_gather | solution.py:51
  62.7 2.2 %copy-start.2 = (bf16[2,1024,320]{2,1,0:T(8,128)(2,1)S(1)}, bf16[2,1024,320]{2,1,0:T(8,128)(2,1)}, u32[]{:S(2)}) copy-start(bf16[2,1024,320]{2,1,0:T(8,128)(2,1)} %copy.49) | copy-start | bytes 3932164
  64.9 6.2 %copy-start.11 = (f32[960]{0:T(1024)S(1)}, f32[960]{0:T(1024)}, u32[]{:S(2)}) copy-start(f32[960]{0:T(1024)} %param.22) | copy-start | bytes 11524
  64.9 6.2 %copy-start.12 = (f32[960]{0:T(1024)S(1)}, f32[960]{0:T(1024)}, u32[]{:S(2)}) copy-start(f32[960]{0:T(1024)} %param.21) | copy-start | bytes 11524
  71.1 6.9 %copy-start.3 = (bf16[2,1024,320]{2,1,0:T(8,128)(2,1)S(1)}, bf16[2,1024,320]{2,1,0:T(8,128)(2,1)}, u32[]{:S(2)}) copy-start(bf16[2,1024,320]{2,1,0:T(8,128)(2,1)} %copy.49) | copy-start | bytes 3932164
  105.8 4.1 %copy-start.6 = (bf16[2,32,32,960]{3,2,1,0:T(8,128)(2,1)S(1)}, bf16[2,32,32,960]{3,2,1,0:T(8,128)(2,1)}, u32[]{:S(2)}) copy-start(bf16[2,32,32,960]{3,2,1,0:T(8,128)(2,1)} %get-tuple-element.6) | copy-start | bytes 11796484
  105.8 6.9 %slice-start = ((s8[5898240]{0:T(1024)(128)(4,1)}), s8[4194304]{0:T(1024)(128)(4,1)S(1)}, s32[]{:S(2)}) async-start(s8[5898240]{0:T(1024)(128)(4,1)} %bitcast.89), calls=%async_computation.2 | async-start | bytes 8388608
  109.9 2.9 %copy-start.5 = (bf16[2,32,32,960]{3,2,1,0:T(8,128)(2,1)S(1)}, bf16[2,32,32,960]{3,2,1,0:T(8,128)(2,1)}, u32[]{:S(2)}) copy-start(bf16[2,32,32,960]{3,2,1,0:T(8,128)(2,1)} %get-tuple-element.7) | copy-start | bytes 11796484
  109.9 3.0 %slice-start.1 = ((s8[5898240]{0:T(1024)(128)(4,1)}), s8[1703936]{0:T(1024)(128)(4,1)S(1)}, s32[]{:S(2)}) async-start(s8[5898240]{0:T(1024)(128)(4,1)} %bitcast.89), calls=%async_computation.3 | async-start | bytes 3407872
  112.9 2.2 %copy-start.4 = (bf16[2,32,32,960]{3,2,1,0:T(8,128)(2,1)S(1)}, bf16[2,32,32,960]{3,2,1,0:T(8,128)(2,1)}, u32[]{:S(2)}) copy-start(bf16[2,32,32,960]{3,2,1,0:T(8,128)(2,1)} %get-tuple-element.8) | copy-start | bytes 11796484
  115.1 2.2 %copy-start.8 = (bf16[2,32,32,960]{3,2,1,0:T(8,128)(2,1)S(1)}, bf16[2,32,32,960]{3,2,1,0:T(8,128)(2,1)}, u32[]{:S(2)}) copy-start(bf16[2,32,32,960]{3,2,1,0:T(8,128)(2,1)} %get-tuple-element.9) | copy-start | bytes 11796484
  117.3 3.1 %copy-start.7 = (bf16[2,1024,960]{2,1,0:T(8,128)(2,1)S(1)}, bf16[2,1024,960]{2,1,0:T(8,128)(2,1)}, u32[]{:S(2)}) copy-start(bf16[2,1024,960]{2,1,0:T(8,128)(2,1)} %multiply_convert_fusion) | copy-start | bytes 11796484
  127.2 1.9 %copy-start.15 = (bf16[960,320]{0,1:T(8,128)(2,1)S(1)}, bf16[960,320]{0,1:T(8,128)(2,1)}, u32[]{:S(2)}) copy-start(bf16[960,320]{0,1:T(8,128)(2,1)} %param.20) | copy-start | bytes 1843204
  129.1 6.2 %copy-start.13 = (f32[320]{0:T(512)S(1)}, f32[320]{0:T(512)}, u32[]{:S(2)}) copy-start(f32[320]{0:T(512)} %param.23) | copy-start | bytes 3844
  135.3 6.0 %copy-start.1 = (bf16[16,128,640]{2,1,0:T(8,128)(2,1)S(1)}, bf16[16,128,640]{2,1,0:T(8,128)(2,1)}, u32[]{:S(2)}) copy-start(bf16[16,128,640]{2,1,0:T(8,128)(2,1)} %param.13) | copy-start | bytes 7864324
Sparse Core Ops, SparseCore 0:
  22.0 60.5 all-gather.1
where the time goes:
time: 149 us; the launch traced here: 148 us
  blocking collectives  38.7 us (26%)
  local copies, waits for them, and re-layouts  35.9 us (24%)
  matrix products  34.4 us (23%)
  other arithmetic  18.8 us (13%)
  between operations  14.4 us (10%)
  starting transfers between devices  5.35 us (4%)
    all_gather x1, blocking collectives, local(): up_portion = lax.all_gather(adapter_up_weight, 'lib', axis=0, tiled=True)  29.5 us
    slice x1, local copies, waits for them, and re-layouts, local(): padded[:, row_off:row_off + ROWS, col_off:col_off + LAT_W]  22.2 us
    dot_general x9, matrix products, local(): jnp.dot(window, kernel_weight[row_off, col_off], preferred_element_type=j...  21.7 us
    convert_element_type x2, other arithmetic, norm_silu(): return jax.nn.silu(scaled).astype(jnp.bfloat16)  12.4 us
    unnamed x1, blocking collectives  9.15 us
    dot_general x1, matrix products, local(): jnp.einsum('rpk,rko->rpo', low, up_blocks, preferred_element_type=jnp.flo...  5.97 us
    gather x2, local copies, waits for them, and re-layouts, local(): outgoing = cached_deep_features[order]  5.97 us
    all_to_all x1, starting transfers between devices, local(): lax.all_to_all(outgoing, 'batch', split_axis=1, concat_axis=1, tiled=True)  5.31 us
  transfers between devices with their start and end apart: 2, of which 0 were waited for; matrix products, arithmetic and copies ran while one was open for 48% of the time, Pallas kernels for 0%

commit v1 on v0

--- a/solution.py
+++ b/solution.py
@@ -2,6 +2,7 @@
 import jax.numpy as jnp
 from jax import lax
 from jax.sharding import PartitionSpec as P
+from jax.lax import axis_index, axis_size, ppermute
 
 DEEP = 640
 GROUPS = 32
@@ -49,7 +50,20 @@
     arrived = lax.all_to_all(outgoing, "batch", split_axis=1, concat_axis=1, tiled=True)
     deep = arrived.reshape(per_device, places, DEEP)
     down_portion = lax.all_gather(adapter_down_weight, "lib", axis=0, tiled=True)
-    up_portion = lax.all_gather(adapter_up_weight, "lib", axis=0, tiled=True)
+    n_all = axis_size("lib")
+    sides = []
+    for ii in [*range(n_all)]:
+        sides.append((ii, (ii + 1) % n_all))
+    fields = []
+    for ii in [*range(n_all)]:
+        fields.append((ii, (ii - 1) % n_all))
+    met_up, moved = ([adapter_up_weight], [adapter_up_weight])
+    for _ in range(n_all // 2):
+        met_up.append(ppermute(met_up[-1], axis_name="lib", perm=sides))
+    for _ in tuple(range((n_all - 1) // 2)):
+        moved.append(ppermute(moved[-1], axis_name="lib", perm=fields))
+    later = jnp.concatenate([*met_up[::-1], *moved[1:]], 0)
+    up_portion = jnp.roll(later, (axis_index("lib") - n_all // 2) * adapter_up_weight.shape[0], 0)
     id_piece = lax.all_gather(library_adapter, "lib", axis=0, tiled=True)
     picker = (request_adapter[:, None] == id_piece[None, :]).astype(jnp.bfloat16)
     down_sum = jnp.einsum("rk,kij->rij", picker, down_portion, preferred_element_type=jnp.float32)

time: 149 us -> 140 us (0.940)
  blocking collectives: 38.7 us -> 11.7 us
  waiting for transfers between devices: 0.68 us -> 10.5 us
  starting transfers between devices: 5.35 us -> 9.77 us
  local copies, waits for them, and re-layouts: 35.9 us -> 38.2 us
  other arithmetic: 18.8 us -> 20.5 us
    all_gather x1 -> x0, blocking collectives: 29.5 us -> none  [local(): up_portion = lax.all_gather(adapter_up_weight, 'lib', axis=0, tiled=True)]
    ppermute x0 -> x3, waiting for transfers between devices: none -> 5.65 us  [the longest x2 5.64 us: local(): met_up.append(ppermute(met_up[-1], axis_name='lib', perm=sides))]
    all_to_all x1, waiting for transfers between devices: 0.01 us -> 4.84 us  [local(): lax.all_to_all(outgoing, 'batch', split_axis=1, concat_axis=1, tiled=True)]
    ppermute x0 -> x3, starting transfers between devices: none -> 4.43 us  [the longest x2 2.34 us: local(): met_up.append(ppermute(met_up[-1], axis_name='lib', perm=sides))]
    unnamed x1, blocking collectives: 9.15 us -> 11.7 us
    concatenate x0 -> x1, local copies, waits for them, and re-layouts: none -> 1.97 us  [local(): jnp.roll(later, (axis_index('lib') - n_all // 2) * adapter_up_weight.shap...]
    reduce_sum x2, other arithmetic: 1.82 us -> 3.51 us  [norm_silu(): center = jnp.mean(values, axis=(1, 3), keepdims=True)]
  transfers between devices with their start and end apart: 2 -> 5, of which waited for: 0 -> 2; matrix products, arithmetic and copies ran while one was open for 48% -> 54% of each run, Pallas kernels for 0% -> 0%
where the time goes in v1:
time: 140 us; the launch traced here: 139 us
  local copies, waits for them, and re-layouts  38.2 us (27%)
  matrix products  34.2 us (24%)
  other arithmetic  20.5 us (15%)
  between operations  14.4 us (10%)
  blocking collectives  11.7 us (8%)
  waiting for transfers between devices  10.5 us (8%)
  starting transfers between devices  9.77 us (7%)
    slice x1, local copies, waits for them, and re-layouts, local(): padded[:, row_off:row_off + ROWS, col_off:col_off + LAT_W]  22.5 us
    dot_general x9, matrix products, local(): jnp.dot(window, kernel_weight[row_off, col_off], preferred_element_type=j...  21.7 us
    convert_element_type x2, other arithmetic, norm_silu(): return jax.nn.silu(scaled).astype(jnp.bfloat16)  12.4 us
    unnamed x1, blocking collectives  11.7 us
    gather x2, local copies, waits for them, and re-layouts, local(): outgoing = cached_deep_features[order]  6.01 us
    dot_general x1, matrix products, local(): jnp.einsum('rpk,rko->rpo', low, up_blocks, preferred_element_type=jnp.flo...  5.96 us
    ppermute x2, waiting for transfers between devices, local(): met_up.append(ppermute(met_up[-1], axis_name='lib', perm=sides))  5.64 us
    all_to_all x1, starting transfers between devices, local(): lax.all_to_all(outgoing, 'batch', split_axis=1, concat_axis=1, tiled=True)  5.3 us
  transfers between devices with their start and end apart: 5, of which 2 were waited for; matrix products, arithmetic and copies ran while one was open for 54% of the time, Pallas kernels for 0%

profile of v1, /device:TPU:0, one launch (start us, length us, event | category | flops | bytes accessed | tf_op | source)
XLA Modules:
  0.0 139.2 jit_solution(13230875354458626727)
XLA Ops:
  6.5 0.8 fusion.48
  7.3 0.6 scatter_custom_fusion
  8.0 0.1 reshape.168
  8.1 0.1 copy.36
  8.1 0.1 reshape.181
  8.2 0.1 copy-done
  8.3 2.4 %gather_fusion = bf16[16,128,640]{2,1,0:T(8,128)(2,1)} fusion(bf16[16,128,640]{2,1,0:T(8,128)(2,1)S(1)} %copy-done, s32[1024]{0:T(1024)S(1)} %pad_clamp_fusion), kind=kCustom, calls=%fused_computation | custom fusion | bytes 5242944 | tf_op jit(solution)/shard_map/gather | solution.py:49
  10.7 3.6 %copy.37 = bf16[2,8,128,640]{3,2,0,1:T(8,128)(2,1)} copy(bf16[2,8,128,640]{3,2,1,0:T(8,128)(2,1)} %bitcast.86) | data formatting | bytes 5242880 | tf_op jit(solution)/shard_map/gather | solution.py:49
  14.3 5.3 %all-to-all-start = ((bf16[2,8,128,640]{3,2,0,1:T(8,128)(2,1)}), bf16[2,8,128,640]{3,2,0,1:T(8,128)(2,1)}, u32[]{:S(2)}, u32[]{:S(2)}) async-start(bf16[2,8,128,640]{3,2,0,1:T(8,128)(2,1)} %copy.37), calls=%async_computation | async-start | bytes 5242880 | tf_op jit(solution)/shard_map/all_to_all | solution.py:50
  19.6 0.0 all-gather.2.cloned.1.call-start
  19.7 0.2 copy.49
  19.8 2.3 %collective-permute-start = (bf16[4,64,320]{2,0,1:T(4,128)(2,1)S(1)}, bf16[4,64,320]{2,0,1:T(4,128)(2,1)S(1)}, u32[]{:S(2)}, u32[]{:S(2)}) collective-permute-start(bf16[4,64,320]{2,0,1:T(4,128)(2,1)S(1)} %copy.49), channel_id=1, source_target_pairs={{0,1},{1,2},{2,3},{3,0},{4,5},{5,6},{6,7},{7,4},{8,9},{9,10},{10,1... | collective-permute-start | bytes 491528 | tf_op jit(solution)/shard_map/ppermute | solution.py:62
  22.2 2.1 %collective-permute-start.2 = (bf16[4,64,320]{2,0,1:T(4,128)(2,1)S(1)}, bf16[4,64,320]{2,0,1:T(4,128)(2,1)S(1)}, u32[]{:S(2)}, u32[]{:S(2)}) collective-permute-start(bf16[4,64,320]{2,0,1:T(4,128)(2,1)S(1)} %copy.49), channel_id=1, source_target_pairs={{0,3},{1,0},{2,1},{3,2},{4,7},{5,4},{6,5},{7,6},{8,11},{9,8},{10,9... | collective-permute-start | bytes 491528 | tf_op jit(solution)/shard_map/ppermute | solution.py:64
  24.3 5.6 %collective-permute-done = bf16[4,64,320]{2,0,1:T(4,128)(2,1)S(1)} collective-permute-done((bf16[4,64,320]{2,0,1:T(4,128)(2,1)S(1)}, bf16[4,64,320]{2,0,1:T(4,128)(2,1)S(1)}, u32[]{:S(2)}, u32[]{:S(2)}) %collective-permute-start) | collective-permute-done | bytes 163872 | tf_op jit(solution)/shard_map/ppermute | solution.py:62
  29.9 0.0 collective-permute-start.1
  29.9 0.0 all-gather.2.cloned.1.call-update
  30.0 1.6 %copy.55 = bf16[2,1024,320]{2,1,0:T(8,128)(2,1)} copy(bf16[2,1024,320]{1,2,0:T(8,128)(2,1)S(1)} %copy-done.8) | data formatting | bytes 2621440 | tf_op jit(solution)/shard_map/concatenate | solution.py:74
  31.6 0.6 dynamic-slice
  32.8 0.2 dynamic-update-slice
  33.1 11.7 %all-reduce.1 = s32[16]{0:T(128)S(1)} all-reduce(s32[16]{0:T(128)S(1)} %dynamic-update-slice), channel_id=1, replica_groups=mesh['batch'=8,'lib'=4] {'lib'}, use_global_device_ids=true, to_apply=%add.1 | all-reduce | flops 16 | bytes 128
  44.8 0.0 collective-permute-done.2
  44.8 0.0 collective-permute-done.1
  44.8 2.0 %concatenate.38 = bf16[32,64,320]{2,0,1:T(8,128)(2,1)S(1)} concatenate(bf16[4,64,320]{2,0,1:T(4,128)(2,1)S(1)} %collective-permute-done.1, bf16[4,64,320]{2,0,1:T(4,128)(2,1)S(1)} %collective-permute-done, bf16[4,64,320]{2,0,1:T(4,128)(2,1)S(1)} %copy.49, bf16[4,64,320]{2,0,1:T(4,128)(2,1)S(1)} %collective-permute-done.2, bf16[4,64,320]{2,0,1:T(4,128)(2,1)S(1)} %collective-permute-done.1, ...), dimensions={0} | concatenate | bytes 2621440 | tf_op jit(solution)/shard_map/jit(_roll_dynamic)/concatenate | solution.py:66
  46.8 0.4 convolution_convert_fusion.1
  47.1 4.8 %all-to-all-done = bf16[2,8,128,640]{3,2,0,1:T(8,128)(2,1)} async-done(((bf16[2,8,128,640]{3,2,0,1:T(8,128)(2,1)}), bf16[2,8,128,640]{3,2,0,1:T(8,128)(2,1)}, u32[]{:S(2)}, u32[]{:S(2)}) %all-to-all-start) | async-done | bytes 2621472 | tf_op jit(solution)/shard_map/all_to_all | solution.py:50
  52.0 2.1 %copy.38 = bf16[2,8,128,640]{3,2,1,0:T(8,128)(2,1)S(1)} copy(bf16[2,8,128,640]{3,2,0,1:T(8,128)(2,1)} %all-to-all-done) | data formatting | bytes 5242880 | tf_op jit(solution)/shard_map/all_to_all | solution.py:50
  54.1 0.0 copy-start.10
  54.1 0.0 copy-start.11
  54.1 3.4 %convert_reduce_fusion = f32[2,960]{1,0:T(2,128)S(1)} fusion(bf16[2,1024,640]{2,1,0:T(8,128)(2,1)S(1)} %bitcast.72, bf16[2,1024,320]{2,1,0:T(8,128)(2,1)} %copy.55), kind=kLoop, calls=%fused_computation.3 | loop fusion | flops 9828480 | bytes 3939840 | tf_op jit(solution)/shard_map/reduce_sum | solution.py:18
  57.5 0.1 reduce_sum.24
  57.6 0.1 reduce_sum.25
  57.7 0.1 sub.38
  57.8 0.1 sub.39
  57.9 3.6 %fusion.2 = f32[2,960]{1,0:T(2,128)S(1)} fusion(f32[2,960]{1,0:T(2,128)S(1)} %sub.39, bf16[2,1024,640]{2,1,0:T(8,128)(2,1)S(1)} %bitcast.73, bf16[2,1024,320]{2,1,0:T(8,128)(2,1)} %copy.55), kind=kLoop, calls=%fused_computation.6 | loop fusion | flops 13760640 | bytes 3947520 | tf_op jit(solution)/shard_map/reduce_sum | solution.py:19
  61.5 0.1 reduce_sum.36
  61.6 0.1 reduce_sum.37
  61.7 0.1 div.49
  61.8 0.1 div.50
  62.0 6.8 %multiply_convert_fusion = bf16[2,1024,960]{2,1,0:T(8,128)(2,1)} fusion(f32[960]{0:T(1024)S(1)} %copy-done.10, f32[960]{0:T(1024)S(1)} %copy-done.11, f32[2,960]{1,0:T(2,128)S(1)} %div.50, f32[2,960]{1,0:T(2,128)S(1)} %sub.39, bf16[2,1024,640]{2,1,0:T(8,128)(2,1)S(1)} %bitcast.74, bf16[2,1024,320]{2,1,0:T(8,128)(2,1)} %copy.55), kind=kLoop, calls=%fused_computation.9 | loop fusion | flops 25559040 | bytes 7887360 | tf_op jit(solution)/shard_map/convert_element_type | solution.py:23
  68.8 5.6 %multiply_convert_fusion.1 = bf16[2,32,32,960]{3,2,1,0:T(8,128)(2,1)} fusion(bf16[2,32,32,640]{3,2,1,0:T(8,128)(2,1)S(1)} %bitcast.75, bf16[2,32,32,320]{3,2,1,0:T(8,128)(2,1)S(1)} %bitcast.77, f32[960]{0:T(1024)S(1)} %copy-done.10, f32[960]{0:T(1024)S(1)} %copy-done.11, f32[2,960]{1,0:T(2,128)S(1)} %div.50, f32[2,960]{1,0:T(2,128)S(1)} %sub.39), kind=kLoop, calls=%fused_computation.10 | loop fusion | flops 25559040 | bytes 7887360 | tf_op jit(solution)/shard_map/convert_element_type | solution.py:23
  74.4 22.5 %pad_slice_fusion = (bf16[2,32,32,960]{3,2,1,0:T(8,128)(2,1)S(1)}, bf16[2,32,32,960]{3,2,1,0:T(8,128)(2,1)}, bf16[2,32,32,960]{3,2,1,0:T(8,128)(2,1)}, bf16[2,32...) fusion(bf16[2,32,32,960]{3,2,1,0:T(8,128)(2,1)} %multiply_conve, ...), kind=kLoop, calls=%fused_computation.11 | loop fusion | bytes 35389440 | tf_op jit(solution)/shard_map/slice | solution.py:82
  96.9 0.0 slice-start
  97.0 4.0 %fusion.30 = f32[2048,320]{0,1:T(8,128)S(1)} fusion(bf16[2048,960]{1,0:T(8,128)(2,1)} %bitcast.88, bf16[3,3,960,320]{2,3,1,0:T(8,128)(2,1)} %param.19), kind=kOutput, calls=%fused_computation.51 | convolution fusion | flops 1258291200 | bytes 7471104 | tf_op jit(solution)/shard_map/dot_general | solution.py:85
  101.0 0.0 slice-start.1
  101.0 2.8 %convolution_add_fusion.6 = f32[2048,320]{0,1:T(8,128)S(1)} fusion(f32[2048,320]{0,1:T(8,128)S(1)} %fusion.30, bf16[2048,960]{1,0:T(8,128)(2,1)S(1)} %bitcast.84, bf16[3,3,960,320]{2,3,1,0:T(8,128)(2,1)} %param.19), kind=kOutput, calls=%fused_computation.32 | convolution fusion | flops 1258946560 | bytes 9830400 | tf_op jit(solution)/shard_map/dot_general | solution.py:85
  103.9 0.0 slice-done
  103.9 0.0 copy-done.4
  103.9 0.2 slice-done.1
  104.1 1.6 %convolution_add_fusion.5 = f32[2048,320]{0,1:T(8,128)S(1)} fusion(f32[2048,320]{0,1:T(8,128)S(1)} %convolution_add_fusion.6, bf16[2048,960]{1,0:T(8,128)(2,1)S(1)} %bitcast.83, bf16[3,3,960,320]{2,3,1,0:T(8,128)(2,1)S(1)} %bitcast.90), kind=kOutput, calls=%fused_computation.31 | convolution fusion | flops 1258946560 | bytes 10092544 | tf_op jit(solution)/shard_map/dot_general | solution.py:85
  105.7 0.6 copy-done.3
  106.3 1.6 %convolution_add_fusion.4 = f32[2048,320]{0,1:T(8,128)S(1)} fusion(f32[2048,320]{0,1:T(8,128)S(1)} %convolution_add_fusion.5, bf16[2048,960]{1,0:T(8,128)(2,1)S(1)} %bitcast.82, bf16[3,3,960,320]{2,3,1,0:T(8,128)(2,1)S(1)} %bitcast.90), kind=kOutput, calls=%fused_computation.30 | convolution fusion | flops 1258946560 | bytes 10092544 | tf_op jit(solution)/shard_map/dot_general | solution.py:85
  107.8 0.6 copy-done.7
  108.5 3.1 %fusion.24 = f32[2048,320]{0,1:T(8,128)} fusion(bf16[2048,960]{1,0:T(8,128)(2,1)S(1)} %bitcast.87, bf16[3,3,960,320]{2,3,1,0:T(8,128)(2,1)S(1)} %bitcast.90), kind=kOutput, calls=%fused_computation.45 | convolution fusion | flops 1258291200 | bytes 7471104 | tf_op jit(solution)/shard_map/dot_general | solution.py:85
  111.6 0.0 copy-done.6
  111.6 3.5 %fusion.12 = f32[2048,320]{0,1:T(8,128)S(1)} fusion(f32[2048,320]{0,1:T(8,128)} %fusion.24, f32[2048,320]{0,1:T(8,128)S(1)} %convolution_add_fusion.4, bf16[2048,960]{1,0:T(8,128)(2,1)S(1)} %bitcast.85, bf16[3,3,960,320]{2,3,1,0:T(8,128)(2,1)S(1)} %bitcast.90), kind=kOutput, calls=%fused_computation.26 | convolution fusion | flops 1259601920 | bytes 12713984 | tf_op jit(solution)/shard_map/dot_general | solution.py:85
  115.0 1.6 %convolution_add_fusion.3 = f32[2048,320]{0,1:T(8,128)S(1)} fusion(f32[2048,320]{0,1:T(8,128)S(1)} %fusion.12, bf16[2048,960]{1,0:T(8,128)(2,1)S(1)} %bitcast.81, bf16[3,3,960,320]{2,3,1,0:T(8,128)(2,1)S(1)} %bitcast.90), kind=kOutput, calls=%fused_computation.29 | convolution fusion | flops 1258946560 | bytes 10092544 | tf_op jit(solution)/shard_map/dot_general | solution.py:85
  116.7 1.6 %convolution_add_fusion.2 = f32[2048,320]{0,1:T(8,128)S(1)} fusion(f32[2048,320]{0,1:T(8,128)S(1)} %convolution_add_fusion.3, bf16[2048,960]{1,0:T(8,128)(2,1)S(1)} %bitcast.80, bf16[3,3,960,320]{2,3,1,0:T(8,128)(2,1)S(1)} %bitcast.90), kind=kOutput, calls=%fused_computation.28 | convolution fusion | flops 1258946560 | bytes 10092544 | tf_op jit(solution)/shard_map/dot_general | solution.py:85
  118.3 0.0 copy-start.14
  118.3 1.9 %convolution_add_fusion.1 = f32[2048,320]{0,1:T(8,128)S(1)} fusion(f32[2048,320]{0,1:T(8,128)S(1)} %convolution_add_fusion.2, bf16[2048,960]{1,0:T(8,128)(2,1)S(1)} %bitcast.79, bf16[3,3,960,320]{2,3,1,0:T(8,128)(2,1)S(1)} %bitcast.90), kind=kOutput, calls=%fused_computation.27 | convolution fusion | flops 1258946560 | bytes 10092544 | tf_op jit(solution)/shard_map/dot_general | solution.py:85
  120.2 0.0 copy-start.12
  120.2 3.3 %fusion.9 = f32[2048,320]{0,1:T(8,128)} fusion(f32[2048,320]{0,1:T(8,128)S(1)} %convolution_add_fusion.1, bf16[960,320]{0,1:T(8,128)(2,1)S(1)} %copy-done.14, bf16[2048,640]{1,0:T(8,128)(2,1)S(1)} %bitcast.76, bf16[2048,320]{1,0:T(8,128)(2,1)S(1)} %bitcast.78), kind=kOutput, calls=%fused_computation.24 | convolution fusion | flops 1266810880 | bytes 9789440 | tf_op jit(solution)/shard_map/dot_general | solution.py:88
  123.5 2.9 %fusion.17 = bf16[2,64,960]{2,0,1:T(2,128)(2,1)S(1)} fusion(bf16[16,64,960]{2,1,0:T(8,128)(2,1)} %all-gather.2.cloned.1.call-done, s32[16]{0:T(128)S(1)} %all-reduce.1, s32[2]{0:T(128)S(1)} %copy-done.13), kind=kOutput, calls=%fused_computation.39 | convolution fusion | flops 4055072 | bytes 2211912 | tf_op jit(solution)/shard_map/rk,kij->rij/dot_general | solution.py:69
  126.4 0.0 copy-start.1
  126.4 6.0 %fusion.14 = bf16[2,1024,320]{1,2,0:T(8,128)(2,1)} fusion(f32[40,2,8,1024]{3,2,1,0:T(8,128)} %bitcast.91, f32[320]{0:T(512)S(1)} %copy-done.12, bf16[2,1024,960]{2,1,0:T(8,128)(2,1)} %multiply_convert_fusion, bf16[2,64,960]{2,0,1:T(2,128)(2,1)S(1)} %fusion.17, bf16[2,64,320]{2,0,1:T(2,128)(2,1)S(1)} %convolution_convert_fusion.1), kind=kOutput, calls=%fused_computation.35 | convolution fusion | flops 337641472 | bytes 8193280 | tf_op jit(solution)/shard_map/rpk,rko->rpo/dot_general | solution.py:96
  (32 shorter events, 0.1 us)
Async XLA Ops:
  6.5 1.8 %copy-start = (bf16[16,128,640]{2,1,0:T(8,128)(2,1)S(1)}, bf16[16,128,640]{2,1,0:T(8,128)(2,1)}, u32[]{:S(2)}) copy-start(bf16[16,128,640]{2,1,0:T(8,128)(2,1)} %param.13) | copy-start | bytes 7864324
  10.7 9.0 %copy-start.9 = (bf16[4,64,320]{2,1,0:T(8,128)(2,1)S(1)}, bf16[4,64,320]{2,1,0:T(8,128)(2,1)}, u32[]{:S(2)}) copy-start(bf16[4,64,320]{2,1,0:T(8,128)(2,1)} %param.18) | copy-start | bytes 491524
  14.3 15.7 %copy-start.8 = (bf16[2,1024,320]{1,2,0:T(8,128)(2,1)S(1)}, bf16[2,1024,320]{1,2,0:T(8,128)(2,1)}, u32[]{:S(2)}) copy-start(bf16[2,1024,320]{1,2,0:T(8,128)(2,1)} %param.12) | copy-start | bytes 3932164
  14.3 17.3 %copy-start.16 = (u32[32]{0:T(128)S(1)}, u32[32]{0:T(128)}, u32[]{:S(2)}) copy-start(u32[32]{0:T(128)} %constant.56) | copy-start | bytes 388
  14.3 18.5 %copy-start.15 = (s32[4]{0:T(128)S(1)}, s32[4]{0:T(128)}, u32[]{:S(2)}) copy-start(s32[4]{0:T(128)} %param.16) | copy-start | bytes 52
  14.3 37.7 %all-to-all-start = ((bf16[2,8,128,640]{3,2,0,1:T(8,128)(2,1)}), bf16[2,8,128,640]{3,2,0,1:T(8,128)(2,1)}, u32[]{:S(2)}, u32[]{:S(2)}) async-start(bf16[2,8,128,640]{3,2,0,1:T(8,128)(2,1)} %copy.37), calls=%async_computation | async-start | bytes 5242880 | tf_op jit(solution)/shard_map/all_to_all | solution.py:50
  19.6 27.2 %copy-start.13 = (s32[2]{0:T(128)S(1)}, s32[2]{0:T(128)}, u32[]{:S(2)}) copy-start(s32[2]{0:T(128)} %param.15) | copy-start | bytes 28
  19.6 103.9 %all-gather.2.cloned.1.call-start = ((), (), s32[]{:S(2)}) async-start(), calls=%async_computation.1 | async-start | bytes 2621440 | tf_op jit(solution)/shard_map/all_gather | solution.py:52
  19.8 10.1 %collective-permute-start = (bf16[4,64,320]{2,0,1:T(4,128)(2,1)S(1)}, bf16[4,64,320]{2,0,1:T(4,128)(2,1)S(1)}, u32[]{:S(2)}, u32[]{:S(2)}) collective-permute-start(bf16[4,64,320]{2,0,1:T(4,128)(2,1)S(1)} %copy.49), channel_id=1, source_target_pairs={{0,1},{1,2},{2,3},{3,0},{4,5},{5,6},{6,7},{7,4},{8,9},{9,10},{10,1... | collective-permute-start | bytes 491528 | tf_op jit(solution)/shard_map/ppermute | solution.py:62
  22.2 22.6 %collective-permute-start.2 = (bf16[4,64,320]{2,0,1:T(4,128)(2,1)S(1)}, bf16[4,64,320]{2,0,1:T(4,128)(2,1)S(1)}, u32[]{:S(2)}, u32[]{:S(2)}) collective-permute-start(bf16[4,64,320]{2,0,1:T(4,128)(2,1)S(1)} %copy.49), channel_id=1, source_target_pairs={{0,3},{1,0},{2,1},{3,2},{4,7},{5,4},{6,5},{7,6},{8,11},{9,8},{10,9... | collective-permute-start | bytes 491528 | tf_op jit(solution)/shard_map/ppermute | solution.py:64
  29.9 14.9 %collective-permute-start.1 = (bf16[4,64,320]{2,0,1:T(4,128)(2,1)S(1)}, bf16[4,64,320]{2,0,1:T(4,128)(2,1)S(1)}, u32[]{:S(2)}, u32[]{:S(2)}) collective-permute-start(bf16[4,64,320]{2,0,1:T(4,128)(2,1)S(1)} %collective-permute-done), channel_id=1, source_target_pairs={{0,1},{1,2},{2,3},{3,0},{4,5},{5,6},{6,7},{7,4},{8,9},{9,10},{10,1... | collective-permute-start | bytes 491528 | tf_op jit(solution)/shard_map/ppermute | solution.py:62
  54.1 7.9 %copy-start.10 = (f32[960]{0:T(1024)S(1)}, f32[960]{0:T(1024)}, u32[]{:S(2)}) copy-start(f32[960]{0:T(1024)} %param.22) | copy-start | bytes 11524
  54.1 7.9 %copy-start.11 = (f32[960]{0:T(1024)S(1)}, f32[960]{0:T(1024)}, u32[]{:S(2)}) copy-start(f32[960]{0:T(1024)} %param.21) | copy-start | bytes 11524
  62.0 6.9 %copy-start.2 = (bf16[2,1024,320]{2,1,0:T(8,128)(2,1)S(1)}, bf16[2,1024,320]{2,1,0:T(8,128)(2,1)}, u32[]{:S(2)}) copy-start(bf16[2,1024,320]{2,1,0:T(8,128)(2,1)} %copy.55) | copy-start | bytes 3932164
  96.9 4.1 %copy-start.5 = (bf16[2,32,32,960]{3,2,1,0:T(8,128)(2,1)S(1)}, bf16[2,32,32,960]{3,2,1,0:T(8,128)(2,1)}, u32[]{:S(2)}) copy-start(bf16[2,32,32,960]{3,2,1,0:T(8,128)(2,1)} %get-tuple-element.6) | copy-start | bytes 11796484
  96.9 6.9 %slice-start = ((s8[5898240]{0:T(1024)(128)(4,1)}), s8[4194304]{0:T(1024)(128)(4,1)S(1)}, s32[]{:S(2)}) async-start(s8[5898240]{0:T(1024)(128)(4,1)} %bitcast.89), calls=%async_computation.2 | async-start | bytes 8388608
  101.0 2.9 %copy-start.4 = (bf16[2,32,32,960]{3,2,1,0:T(8,128)(2,1)S(1)}, bf16[2,32,32,960]{3,2,1,0:T(8,128)(2,1)}, u32[]{:S(2)}) copy-start(bf16[2,32,32,960]{3,2,1,0:T(8,128)(2,1)} %get-tuple-element.7) | copy-start | bytes 11796484
  101.0 3.0 %slice-start.1 = ((s8[5898240]{0:T(1024)(128)(4,1)}), s8[1703936]{0:T(1024)(128)(4,1)S(1)}, s32[]{:S(2)}) async-start(s8[5898240]{0:T(1024)(128)(4,1)} %bitcast.89), calls=%async_computation.3 | async-start | bytes 3407872
  104.1 2.2 %copy-start.3 = (bf16[2,32,32,960]{3,2,1,0:T(8,128)(2,1)S(1)}, bf16[2,32,32,960]{3,2,1,0:T(8,128)(2,1)}, u32[]{:S(2)}) copy-start(bf16[2,32,32,960]{3,2,1,0:T(8,128)(2,1)} %get-tuple-element.8) | copy-start | bytes 11796484
  106.3 2.2 %copy-start.7 = (bf16[2,32,32,960]{3,2,1,0:T(8,128)(2,1)S(1)}, bf16[2,32,32,960]{3,2,1,0:T(8,128)(2,1)}, u32[]{:S(2)}) copy-start(bf16[2,32,32,960]{3,2,1,0:T(8,128)(2,1)} %get-tuple-element.9) | copy-start | bytes 11796484
  108.5 3.1 %copy-start.6 = (bf16[2,1024,960]{2,1,0:T(8,128)(2,1)S(1)}, bf16[2,1024,960]{2,1,0:T(8,128)(2,1)}, u32[]{:S(2)}) copy-start(bf16[2,1024,960]{2,1,0:T(8,128)(2,1)} %multiply_convert_fusion) | copy-start | bytes 11796484
  118.3 1.9 %copy-start.14 = (bf16[960,320]{0,1:T(8,128)(2,1)S(1)}, bf16[960,320]{0,1:T(8,128)(2,1)}, u32[]{:S(2)}) copy-start(bf16[960,320]{0,1:T(8,128)(2,1)} %param.20) | copy-start | bytes 1843204
  120.2 6.2 %copy-start.12 = (f32[320]{0:T(512)S(1)}, f32[320]{0:T(512)}, u32[]{:S(2)}) copy-start(f32[320]{0:T(512)} %param.23) | copy-start | bytes 3844
  126.4 6.0 %copy-start.1 = (bf16[16,128,640]{2,1,0:T(8,128)(2,1)S(1)}, bf16[16,128,640]{2,1,0:T(8,128)(2,1)}, u32[]{:S(2)}) copy-start(bf16[16,128,640]{2,1,0:T(8,128)(2,1)} %param.13) | copy-start | bytes 7864324
Sparse Core Ops, SparseCore 0:
  30.1 49.3 all-gather.1
